TPU v7x, 32 devices: a whole 2x2x4 slice. The times are simulated.
32 devices in a mesh: page: 4 (over x, core), tensor: 8 (over z, y).
Axes of the slice: x: 2, y: 2, z: 4, core: 2. Of those that a mesh axis runs over, the one named last changes fastest.
Arguments:
- tokens: bfloat16 [512, 2560], P('tensor'), may hold values from -6 to 6
- norm_gain: float32 [2560], replicated, may hold values from 0.1 to 1.9
- w_query: bfloat16 [2560, 2560], P(None, 'tensor'), may hold values from -0.125 to 0.125
- w_keyvalue: bfloat16 [2560, 1280], P(None, 'tensor'), may hold values from -0.125 to 0.125
- cache: bfloat16 [32, 8, 128, 1280], P('page', 'tensor'), may hold values from -180 to 180, as said below
- page_count: int32 [4, 8], P('page', 'tensor'), may hold values from 1 to 8, as said below
- page_owner: int32 [32, 8], P('page', 'tensor'), may hold values from 0 to 63
- keep_rows: int32 [32, 8, 32], P('page', 'tensor'), may hold values from 0 to 127, as said below
- dest_slot: int32 [32, 8], P('page', 'tensor'), may hold values from 0 to 7, as said below
Outputs:
- attended: bfloat16 [512, 2560], P('tensor')
- compacted: bfloat16 [32, 8, 32, 1280], P('page', 'tensor')
Inputs may be any that keep to these rules, and one draw needn't show every extreme that they name: `cache`: normal values within 4.5; keys may carry a row scale. `page_count`: in every tensor index some holder has all 8 slots live. `keep_rows`: distinct within each page. `dest_slot`: value q * 2 * 2 + c names position c of holder q (with 2 = 2, c = 0); the live slots of one holder and tensor index name distinct destinations, and every holder's first slot of a tensor index goes to position 0 of one common holder of that index.
All inputs are finite; a program needn't handle non-finite values.
Results may differ from a plain program's by a relative error of at most 0.012.
Values may be sent and summed in bfloat16 or wider, within the bound.
A program may use at most 64 MiB of HBM per device.

v0:
```python
import jax
import jax.numpy as jnp
from jax import lax
from jax.sharding import PartitionSpec as P

HEADS = 32
KV_HEADS = 8
HEAD_DIM = 80


EPSILON = 1e-05
NEGATIVE = -1e30


def per_device(
    tokens, norm_gain, w_query, w_keyvalue, cache, page_count, page_owner, keep_rows, dest_slot
):
    holders = lax.axis_size("page")
    groups = lax.axis_size("tensor")
    rows_here = tokens.shape[0]
    sources = cache.shape[0]
    keep_count = keep_rows.shape[2]
    row_width = cache.shape[3]
    capacity = (sources + holders - 1) // holders
    targets = capacity * holders
    repeat_count = HEADS // KV_HEADS
    score_scale = HEAD_DIM ** (-0.5)
    widened = tokens.astype(jnp.float32)
    normed = (
        widened
        * lax.rsqrt(jnp.mean(widened * widened, axis=-1, keepdims=True) + EPSILON)
        * norm_gain
    ).astype(jnp.bfloat16)
    portion = lax.all_gather(normed, "tensor", axis=0, tiled=True)
    query_part = jnp.dot(portion, w_query, preferred_element_type=jnp.float32)
    pair_part = jnp.dot(portion, w_keyvalue, preferred_element_type=jnp.float32)
    projected = jnp.concatenate([query_part, pair_part], axis=1).astype(jnp.bfloat16)
    local_heads = lax.all_to_all(
        projected, "tensor", split_axis=0, concat_axis=1, tiled=True
    ).reshape(rows_here, groups, -1)
    query_cols = w_query.shape[1]
    queries = local_heads[:, :, :query_cols].reshape(rows_here, KV_HEADS, repeat_count, HEAD_DIM)
    fresh_kv = local_heads[:, :, query_cols:].reshape(rows_here, 2, KV_HEADS, HEAD_DIM)
    new_keys = fresh_kv[:, 0]
    new_values = fresh_kv[:, 1]
    retained = jax.vmap(lambda one_page, row_picks: one_page[row_picks])(
        cache[:, 0], keep_rows[:, 0]
    )
    is_live = jnp.arange(sources) < page_count[0, 0]
    owners = page_owner[:, 0]
    chosen = (dest_slot[:, 0][None, :] == jnp.arange(targets)[:, None]) & is_live[None, :]
    outgoing = jnp.einsum(
        "ts,sjc->tjc", chosen.astype(jnp.bfloat16), retained, preferred_element_type=jnp.float32
    ).astype(jnp.bfloat16)
    out_tags = jnp.sum(jnp.where(chosen, owners[None, :] + 1, 0), axis=1) - 1
    arrived, arrived_tags = (
        lax.all_to_all(
            outgoing.reshape(holders, capacity, keep_count, row_width),
            "page",
            split_axis=0,
            concat_axis=0,
            tiled=True,
        ),
        lax.all_to_all(
            out_tags.reshape(holders, capacity), "page", split_axis=0, concat_axis=0, tiled=True
        ),
    )
    arrived = arrived.reshape(targets, keep_count, row_width)
    arrived_tags = arrived_tags.reshape(targets)
    slot_count = arrived.shape[0]
    active = arrived_tags >= 0
    owner_idx = jnp.maximum(arrived_tags, 0)
    picked = jnp.take(queries, owner_idx, axis=0)
    slot_keys = arrived[:, :, : KV_HEADS * HEAD_DIM].reshape(
        slot_count, keep_count, KV_HEADS, HEAD_DIM
    )
    slot_values = arrived[:, :, KV_HEADS * HEAD_DIM :].reshape(
        slot_count, keep_count, KV_HEADS, HEAD_DIM
    )
    scores = (
        jnp.einsum("sgkd,sjgd->sgkj", picked, slot_keys, preferred_element_type=jnp.float32)
        * score_scale
    )
    member = (owner_idx[None, :] == jnp.arange(rows_here)[:, None]) & active[None, :]
    slot_peak = jnp.max(scores, axis=3)
    local_peak = jnp.max(jnp.where(member[:, :, None, None], slot_peak[None], NEGATIVE), axis=1)
    own_score = (
        jnp.einsum("rgkd,rgd->rgk", queries, new_keys, preferred_element_type=jnp.float32)
        * score_scale
    )
    row_peak = jnp.maximum(lax.pmax(local_peak, "page"), own_score)
    shifted = scores - jnp.take(row_peak, owner_idx, axis=0)[..., None]
    weights = jnp.where(active[:, None, None, None], jnp.exp(shifted), 0.0)
    slot_total = jnp.sum(weights, axis=3)
    slot_out = jnp.einsum(
        "sgkj,sjgd->sgkd",
        weights.astype(jnp.bfloat16),
        slot_values,
        preferred_element_type=jnp.float32,
    )
    member_weight = member.astype(jnp.float32)
    part_total = jnp.einsum(
        "rs,sgk->rgk", member_weight, slot_total, precision=lax.Precision.HIGHEST
    )
    part_out = jnp.einsum("rs,sgkd->rgkd", member_weight, slot_out, precision=lax.Precision.HIGHEST)
    sum_out, sum_total = lax.psum((part_out, part_total), "page")
    own_weight = jnp.exp(own_score - row_peak)
    mixed = sum_out + own_weight[..., None] * new_values[:, :, None, :].astype(jnp.float32)
    result = mixed / (sum_total + own_weight)[..., None]
    return (result.reshape(rows_here, HEADS * HEAD_DIM).astype(jnp.bfloat16), arrived[:, None])


def solution(mesh):
    return jax.shard_map(
        per_device,
        mesh=mesh,
        in_specs=(
            P("tensor", None),
            P(),
            P(None, "tensor"),
            P(None, "tensor"),
            P("page", "tensor", None, None),
            P("page", "tensor"),
            P("page", "tensor"),
            P("page", "tensor", None),
            P("page", "tensor"),
        ),
        out_specs=(P("tensor", None), P("page", "tensor", None, None)),
        check_vma=False,
    )
```

profile of v0, /device:TPU:0, one launch (start us, length us, event | category | flops | bytes accessed | tf_op | source)
XLA Modules:
  0.0 169.4 jit_solution(1425014296427751171)
XLA Ops:
  7.2 0.0 all-gather.2.cloned.1.call-start
  7.2 1.3 fusion
  8.5 1.9 %fusion.2 = bf16[64,2560]{1,0:T(8,128)(2,1)} fusion(bf16[64,2560]{1,0:T(8,128)(2,1)} %param.9, f32[2560]{0:T(1024)} %param.10, f32[64]{0:T(128)S(1)} %add_rsqrt_fusion), kind=kLoop, calls=%fused_computation.12 | loop fusion | flops 655360 | bytes 665856 | tf_op jit(solution)/shard_map/convert_element_type | solution.py:33
  10.4 0.0 all-gather.2.cloned.1.call-update
  11.1 0.7 add_bitcast_fusion
  11.7 0.8 select_reduce_fusion.1
  12.5 0.7 sub.17
  13.2 4.2 %all-to-all-start = ((s32[4,1,2]{2,1,0:T(1,128)}), s32[4,1,2]{2,1,0:T(1,128)S(1)}, u32[]{:S(2)}, u32[]{:S(2)}) async-start(s32[4,1,2]{2,1,0:T(1,128)} %bitcast.3), calls=%async_computation | async-start | bytes 4096 | tf_op jit(solution)/shard_map/all_to_all | solution.py:64
  17.4 0.7 fusion.22
  18.1 0.1 reshape.213
  18.2 3.2 %gather_fusion.2 = bf16[256,1280]{1,0:T(8,128)(2,1)S(1)} fusion(bf16[8,128,1280]{2,1,0:T(8,128)(2,1)S(1)} %bitcast.54, s32[256]{0:T(256)S(1)} %reshape.213), kind=kCustom, calls=%fused_computation.2 | custom fusion | bytes 1312768 | tf_op jit(solution)/shard_map/vmap()/gather | solution.py:46
  21.4 1.3 convolution_convert_fusion
  22.7 2.0 %reshape.191 = bf16[4,2,32,1280]{3,1,0,2:T(2,128)(2,1)S(1)} reshape(bf16[8,32,1280]{2,0,1:T(8,128)(2,1)} %convolution_convert_fusion) | data formatting | bytes 1310720 | tf_op jit(solution)/shard_map/reshape | solution.py:58
  24.7 1.3 copy.140
  26.0 3.5 %all-to-all-start.2 = ((bf16[4,2,32,1280]{3,1,2,0:T(2,128)(2,1)}), bf16[4,2,32,1280]{3,1,2,0:T(2,128)(2,1)S(1)}, u32[]{:S(2)}, u32[]{:S(2)}) async-start(bf16[4,2,32,1280]{3,1,2,0:T(2,128)(2,1)} %copy.140), calls=%async_computation.2 | async-start | bytes 1310720 | tf_op jit(solution)/shard_map/all_to_all | solution.py:57
  29.5 38.7 %all-gather.2.cloned.1.call-done = bf16[512,2560]{1,0:T(8,128)(2,1)} async-done(((bf16[64,2560]{1,0:T(8,128)(2,1)}), bf16[512,2560]{1,0:T(8,128)(2,1)}) %all-gather.2.cloned.1.call-update) | async-done | bytes 2621456 | tf_op jit(solution)/shard_map/all_gather | solution.py:34
  68.2 4.0 %convolution_convert_fusion.1 = bf16[512,320]{0,1:T(8,128)(2,1)} fusion(bf16[512,2560]{1,0:T(8,128)(2,1)} %all-gather.2.cloned.1.call-done, bf16[2560,320]{0,1:T(8,128)(2,1)} %param.11), kind=kOutput, calls=%fused_computation.4 | convolution fusion | flops 839024640 | bytes 4587520 | tf_op jit(solution)/shard_map/dot_general | solution.py:35
  72.1 1.9 %copy.135 = bf16[512,320]{1,0:T(8,128)(2,1)} copy(bf16[512,320]{0,1:T(8,128)(2,1)} %convolution_convert_fusion.1) | data formatting | bytes 655360 | tf_op jit(solution)/shard_map/convert.4
  74.0 3.6 %convolution_convert_fusion.2 = bf16[512,160]{0,1:T(8,128)(2,1)} fusion(bf16[512,2560]{1,0:T(8,128)(2,1)} %all-gather.2.cloned.1.call-done, bf16[2560,160]{0,1:T(8,128)(2,1)} %param.12), kind=kOutput, calls=%fused_computation.5 | convolution fusion | flops 419512320 | bytes 3604480 | tf_op jit(solution)/shard_map/dot_general | solution.py:36
  77.6 1.0 copy.160
  78.7 2.0 %pad_maximum_fusion = bf16[8,64,480]{2,1,0:T(8,128)(2,1)} fusion(bf16[8,64,160]{2,1,0:T(8,128)(2,1)S(1)} %bitcast.61, bf16[8,64,320]{2,1,0:T(8,128)(2,1)} %bitcast.60), kind=kLoop, calls=%fused_computation.14 | loop fusion | flops 983040 | bytes 983040 | tf_op jit(solution)/shard_map/concatenate | solution.py:37
  80.6 0.8 copy-done.2
  81.5 3.5 %all-to-all-start.1 = ((bf16[8,64,480]{2,1,0:T(8,128)(2,1)}), bf16[8,64,480]{2,1,0:T(8,128)(2,1)S(1)}, u32[]{:S(2)}, u32[]{:S(2)}) async-start(bf16[8,64,480]{2,1,0:T(8,128)(2,1)} %pad_maximum_fusion), calls=%async_computation.1 | async-start | bytes 1048576 | tf_op jit(solution)/shard_map/all_to_all | solution.py:38
  85.0 0.0 all-reduce.2.cloned.1.call-start
  85.0 0.1 ge.22
  85.1 0.1 max.28
  85.2 0.5 broadcast_compare_fusion
  85.8 0.1 fusion.26
  85.8 1.2 copy.141
  87.0 0.8 copy-done.1
  87.8 0.8 fusion.36
  88.6 2.4 %reshape.193 = bf16[8,32,8,80]{3,2,1,0:T(8,128)(2,1)} reshape(bf16[8,32,640]{2,1,0:T(8,128)(2,1)} %get-tuple-element.10) | data formatting | bytes 655360 | tf_op jit(solution)/shard_map/reshape | solution.py:74
  91.0 1.4 reshape.195
  92.4 6.8 %all-to-all-done.1 = bf16[8,64,480]{2,1,0:T(8,128)(2,1)S(1)} async-done(((bf16[8,64,480]{2,1,0:T(8,128)(2,1)}), bf16[8,64,480]{2,1,0:T(8,128)(2,1)S(1)}, u32[]{:S(2)}, u32[]{:S(2)}) %all-to-all-start.1) | async-done | bytes 491552 | tf_op jit(solution)/shard_map/all_to_all | solution.py:38
  99.2 0.1 slice.32
  99.4 0.2 copy.137
  99.6 0.2 copy.145
  99.8 0.9 reshape.194
  100.6 0.3 reshape.190
  101.0 1.0 fusion.9
  102.0 0.9 copy.138
  102.9 1.4 fusion.7
  104.3 1.1 copy.158
  105.4 1.6 gather_fusion
  107.0 0.1 broadcast_select_fusion
  107.1 1.5 fusion.37
  108.6 0.1 copy.144
  108.7 0.1 select_reduce_fusion
  108.8 10.3 %pmax.7 = f32[64,8,4]{0,1,2:T(8,128)S(1)} all-reduce(f32[64,8,4]{0,1,2:T(8,128)S(1)} %select_reduce_fusion), channel_id=1, replica_groups=mesh['page'=4,'tensor'=8] {'page'}, use_global_device_ids=true, to_apply=%region_4.5 | all-reduce | flops 2048 | bytes 16384 | tf_op jit(solution)/shard_map/pmax | solution.py:91
  119.1 0.1 copy.146
  119.2 0.6 gather_fusion.1
  119.8 0.1 broadcast_select_fusion.1
  119.9 0.1 copy.147
  120.0 0.3 fusion.12
  120.3 0.1 copy.152
  120.4 1.4 fusion.4
  121.8 1.7 %fusion.10 = f32[64,8,4,80]{3,0,2,1:T(8,128)} fusion(f32[8,8,4,80]{3,2,1,0:T(4,128)S(1)} %fusion.4, s32[8]{0:T(128)S(1)} %max.28, pred[8]{0:T(512)(128)(4,1)S(1)} %ge.22), kind=kOutput, calls=%fused_computation.23 | convolution fusion | flops 15729664 | bytes 737320 | tf_op jit(solution)/shard_map/rs,sgkd->rgkd/dot_general | solution.py:105
  123.5 0.2 fusion.28
  123.7 0.1 copy.151
  123.8 10.8 %psum.15 = f32[64,8,4]{0,1,2:T(8,128)S(1)} all-reduce(f32[64,8,4]{0,1,2:T(8,128)S(1)} %fusion.28), channel_id=1, replica_groups=mesh['page'=4,'tensor'=8] {'page'}, use_global_device_ids=true, to_apply=%region_7.8 | all-reduce | flops 2048 | bytes 16384 | tf_op jit(solution)/shard_map/psum | solution.py:106
  134.7 24.2 %all-reduce.2.cloned.1.call-done = f32[64,8,4,80]{3,0,2,1:T(8,128)} async-done(((f32[64,8,4,80]{3,0,2,1:T(8,128)}), f32[64,8,4,80]{3,0,2,1:T(8,128)}) %all-reduce.2.cloned.1.call-update) | async-done | bytes 655376 | tf_op jit(solution)/shard_map/psum | solution.py:106
  158.8 1.8 %divide_convert_fusion = bf16[64,8,4,80]{3,0,2,1:T(8,128)(2,1)S(1)} fusion(f32[64,8,4,80]{3,0,2,1:T(8,128)} %all-reduce.2.cloned.1.call-done, f32[64,8,4]{0,2,1:T(4,128)S(1)} %copy.153, f32[64,8,80]{2,0,1:T(8,128)S(1)} %copy.151, f32[64,8,4]{0,2,1:T(4,128)S(1)} %copy.150), kind=kLoop, calls=%fused_computation.7 | loop fusion | flops 655360 | bytes 1163264 | tf_op jit(solution)/shard_map/convert_element_type | solution.py:110
  160.6 0.4 copy.154
  161.0 1.6 convert_element_type.40
  (22 shorter events, 0.2 us)
Async XLA Ops:
  7.2 11.0 %copy-start = (bf16[8,1,128,1280]{3,2,1,0:T(8,128)(2,1)S(1)}, bf16[8,1,128,1280]{3,2,1,0:T(8,128)(2,1)}, u32[]{:S(2)}) copy-start(bf16[8,1,128,1280]{3,2,1,0:T(8,128)(2,1)} %param.13) | copy-start | bytes 7864324
  7.2 61.0 %all-gather.2.cloned.1.call-start = ((), (), s32[]{:S(2)}) async-start(), calls=%async_computation.3 | async-start | bytes 2949120 | tf_op jit(solution)/shard_map/all_gather | solution.py:34
  13.2 12.8 %all-to-all-start = ((s32[4,1,2]{2,1,0:T(1,128)}), s32[4,1,2]{2,1,0:T(1,128)S(1)}, u32[]{:S(2)}, u32[]{:S(2)}) async-start(s32[4,1,2]{2,1,0:T(1,128)} %bitcast.3), calls=%async_computation | async-start | bytes 4096 | tf_op jit(solution)/shard_map/all_to_all | solution.py:64
  18.2 3.2 %copy-start.4 = (s32[8,1]{0,1:T(1,128)S(1)}, s32[8,1]{0,1:T(1,128)}, u32[]{:S(2)}) copy-start(s32[8,1]{0,1:T(1,128)} %param.17) | copy-start | bytes 100
  26.0 54.7 %all-to-all-start.2 = ((bf16[4,2,32,1280]{3,1,2,0:T(2,128)(2,1)}), bf16[4,2,32,1280]{3,1,2,0:T(2,128)(2,1)S(1)}, u32[]{:S(2)}, u32[]{:S(2)}) async-start(bf16[4,2,32,1280]{3,1,2,0:T(2,128)(2,1)} %copy.140), calls=%async_computation.2 | async-start | bytes 1310720 | tf_op jit(solution)/shard_map/all_to_all | solution.py:57
  80.6 0.8 copy-start.2
  81.5 17.7 %all-to-all-start.1 = ((bf16[8,64,480]{2,1,0:T(8,128)(2,1)}), bf16[8,64,480]{2,1,0:T(8,128)(2,1)S(1)}, u32[]{:S(2)}, u32[]{:S(2)}) async-start(bf16[8,64,480]{2,1,0:T(8,128)(2,1)} %pad_maximum_fusion), calls=%async_computation.1 | async-start | bytes 1048576 | tf_op jit(solution)/shard_map/all_to_all | solution.py:38
  85.0 73.9 %all-reduce.2.cloned.1.call-start = ((), (), s32[]{:S(2)}) async-start(), calls=%async_computation.4 | async-start | bytes 2097152 | tf_op jit(solution)/shard_map/psum | solution.py:106
  87.0 0.8 copy-start.1
  101.0 6.0 %copy-start.3 = (pred[8]{0:T(512)(128)(4,1)S(1)}, pred[8]{0:T(512)(128)(4,1)}, u32[]{:S(2)}) copy-start(pred[8]{0:T(512)(128)(4,1)} %broadcast_compare_fusion) | copy-start | bytes 28
Sparse Core Ops, SparseCore 0:
  10.8 57.3 all-gather.1
  123.7 35.1 all-reduce.1
where the time goes:
time: 170 us; the launch traced here: 169 us
  waiting for transfers between devices  69.7 us (41%)
  local copies, waits for them, and re-layouts  26.1 us (15%)
  blocking collectives  21.1 us (12%)
  matrix products  15.1 us (9%)
  between operations  14.9 us (9%)
  starting transfers between devices  11.3 us (7%)
  other arithmetic  11.2 us (7%)
    all_gather x1, waiting for transfers between devices, per_device(): portion = lax.all_gather(normed, 'tensor', axis=0, tiled=True)  38.7 us
    psum x1, waiting for transfers between devices, per_device(): sum_out, sum_total = lax.psum((part_out, part_total), 'page')  24.2 us
    psum x1, blocking collectives, per_device(): sum_out, sum_total = lax.psum((part_out, part_total), 'page')  10.8 us
    pmax x1, blocking collectives, per_device(): row_peak = jnp.maximum(lax.pmax(local_peak, 'page'), own_score)  10.3 us
    all_to_all x1, waiting for transfers between devices, per_device(): lax.all_to_all(projected, 'tensor', split_axis=0, concat_axis=1, tiled=True)  6.82 us
    all_to_all x1, starting transfers between devices, per_device(): lax.all_to_all(out_tags.reshape(holders, capacity), 'page', split_axis=0,...  4.21 us
    dot_general x1, matrix products, per_device(): query_part = jnp.dot(portion, w_query, preferred_element_type=jnp.float32)  3.98 us
    dot_general x1, matrix products, per_device(): pair_part = jnp.dot(portion, w_keyvalue, preferred_element_type=jnp.float32)  3.59 us
  transfers between devices with their start and end apart: 5, of which 3 were waited for; matrix products, arithmetic and copies ran while one was open for 18% of the time, Pallas kernels for 0%

commit v1 on v0

--- a/solution.py
+++ b/solution.py
@@ -1,6 +1,10 @@
+import functools
+
 import jax
 import jax.numpy as jnp
 from jax import lax
+from jax.experimental import pallas as pl
+from jax.experimental.pallas import tpu as pltpu
 from jax.sharding import PartitionSpec as P
 
 HEADS = 32
@@ -110,9 +114,386 @@
     return (result.reshape(rows_here, HEADS * HEAD_DIM).astype(jnp.bfloat16), arrived[:, None])
 
 
+MESH = pl.DeviceIdType.MESH
+SCALE = HEAD_DIM ** (-0.5)
+REPEAT = HEADS // KV_HEADS
+PLANE = KV_HEADS * HEAD_DIM
+HOLDERS, GROUPS = 4, 8
+
+
+def head_of(shape, axis):
+    return (lax.broadcasted_iota(jnp.int32, shape, axis) * 3277) >> 18
+
+
+def partner(index, flip):
+    for bit in (1, 2, 4):
+        if flip & bit:
+            index = index + bit - 2 * bit * lax.rem(lax.div(index, bit), 2)
+    return index
+
+
+def split_dot(a, b):
+    high = a.astype(jnp.bfloat16)
+    low = (a - high.astype(jnp.float32)).astype(jnp.bfloat16)
+    return jnp.dot(high, b, preferred_element_type=jnp.float32) + jnp.dot(
+        low, b, preferred_element_type=jnp.float32
+    )
+
+
+def exact_dot(a, b):
+    return jnp.dot(a, b, precision=lax.Precision.HIGHEST, preferred_element_type=jnp.float32)
+
+
+def fused_kernel(
+    tokens, gain, code, tags, tag_rows, w_query, w_keyvalue, cache,
+    attended, compacted,
+    wq, wkv, pages, rows, leaving, projected, local, planes, fresh, sums, peaks,
+    load_sem, keep_sem, row_send, row_recv, page_send, page_recv, proj_send, proj_recv,
+    query_send, query_recv, fresh_send, fresh_recv, sum_send, sum_recv, peak_send, peak_recv,
+):
+    p = lax.axis_index("page")
+    t = lax.axis_index("tensor")
+    part = rows.shape[1]
+    requests = part * HOLDERS
+    slots = tags.shape[0]
+    keep = leaving.shape[1]
+    cap = slots // HOLDERS
+    page_rows = cache.shape[0] // slots
+
+    loads = [
+        pltpu.make_async_copy(cache, pages, load_sem.at[0]),
+        pltpu.make_async_copy(w_query, wq, load_sem.at[1]),
+        pltpu.make_async_copy(w_keyvalue, wkv, load_sem.at[2]),
+    ]
+    for load in loads:
+        load.start()
+
+    barrier = pltpu.get_barrier_semaphore()
+    for f in range(1, GROUPS):
+        pl.semaphore_signal(barrier, inc=1, device_id=(p, partner(t, f)), device_id_type=MESH)
+    for f in range(1, HOLDERS):
+        pl.semaphore_signal(barrier, inc=1, device_id=(partner(p, f), t), device_id_type=MESH)
+
+    mine = tokens[p].astype(jnp.float32)
+    square = jnp.mean(mine * mine, axis=-1, keepdims=True)
+    rows[0] = (mine * lax.rsqrt(square + EPSILON) * gain[...]).astype(jnp.bfloat16)
+    pl.semaphore_wait(barrier, GROUPS + HOLDERS - 2)
+
+    def pass_row(e, f):
+        copy = pltpu.make_async_remote_copy(
+            src_ref=rows.at[e],
+            dst_ref=rows.at[e ^ f],
+            send_sem=row_send.at[e ^ f],
+            recv_sem=row_recv.at[e ^ f],
+            device_id=(p, partner(t, f)),
+            device_id_type=MESH,
+        )
+        copy.start()
+        return copy
+
+    moved = {4: pass_row(0, 4), 2: pass_row(0, 2), 1: pass_row(0, 1)}
+
+    loads[0].wait()
+    lane = lax.broadcasted_iota(jnp.int32, (slots * keep, page_rows), 1)
+    code_values = code[...]
+    choice = jnp.concatenate(
+        [jnp.where(code_values[:, s : s + 1] == lane, 1.0, 0.0).astype(jnp.bfloat16) for s in range(slots)],
+        axis=1,
+    )
+    out = jnp.dot(choice, pages[...], preferred_element_type=jnp.float32).astype(jnp.bfloat16)
+    leaving[...] = out.reshape(leaving.shape)
+    page_copies = []
+    for f in range(1, HOLDERS):
+        copy = pltpu.make_async_remote_copy(
+            src_ref=leaving.at[pl.ds(partner(p, f) * cap, cap)],
+            dst_ref=compacted.at[pl.ds(p * cap, cap)],
+            send_sem=page_send.at[f],
+            recv_sem=page_recv.at[f],
+            device_id=(partner(p, f), t),
+            device_id_type=MESH,
+        )
+        copy.start()
+        page_copies.append(copy)
+    kept = pltpu.make_async_copy(
+        leaving.at[pl.ds(p * cap, cap)], compacted.at[pl.ds(p * cap, cap)], keep_sem
+    )
+    kept.start()
+
+    moved[4].wait_recv()
+    moved[6] = pass_row(4, 2)
+    moved[5] = pass_row(4, 1)
+    moved[2].wait_recv()
+    moved[3] = pass_row(2, 1)
+    loads[1].wait()
+    loads[2].wait()
+    moved[6].wait_recv()
+    moved[7] = pass_row(6, 1)
+
+    def project(first):
+        batch = jnp.concatenate([rows[e] for e in range(first, GROUPS, 2)], axis=0)
+        query = jnp.dot(batch, wq[...], preferred_element_type=jnp.float32)
+        pair = jnp.dot(batch, wkv[...], preferred_element_type=jnp.float32)
+        spare = jnp.zeros((batch.shape[0], projected.shape[2] - 480), jnp.float32)
+        both = jnp.concatenate([query, pair, spare], axis=1).astype(jnp.bfloat16)
+        copies = []
+        for n, e in enumerate(range(first, GROUPS, 2)):
+            block = both[n * part : (n + 1) * part]
+            if e == 0:
+                local[t] = block
+                continue
+            projected[e] = block
+            copy = pltpu.make_async_remote_copy(
+                src_ref=projected.at[e],
+                dst_ref=local.at[t],
+                send_sem=proj_send.at[e],
+                recv_sem=proj_recv.at[e],
+                device_id=(p, partner(t, e)),
+                device_id_type=MESH,
+            )
+            copy.start()
+            copies.append(copy)
+        return copies
+
+    proj_copies = project(0)
+    for e in (1, 3, 5, 7):
+        moved[e].wait_recv()
+    proj_copies += project(1)
+    for copy in proj_copies:
+        copy.wait_recv()
+
+    blocks = [local[g].astype(jnp.float32) for g in range(GROUPS)]
+    for k in range(REPEAT):
+        planes[p, k] = jnp.concatenate(
+            [b[:, k * HEAD_DIM : (k + 1) * HEAD_DIM] for b in blocks], axis=1
+        ).astype(jnp.bfloat16)
+    for n in range(2):
+        fresh[p, n] = jnp.concatenate(
+            [b[:, 320:480] for b in blocks[4 * n : 4 * n + 4]], axis=1
+        ).astype(jnp.bfloat16)
+
+    def to_holders(ref_of, send, recv):
+        copies = []
+        for f in range(1, HOLDERS):
+            copy = pltpu.make_async_remote_copy(
+                src_ref=ref_of(),
+                dst_ref=ref_of(),
+                send_sem=send.at[f],
+                recv_sem=recv.at[f],
+                device_id=(partner(p, f), t),
+                device_id_type=MESH,
+            )
+            copy.start()
+            copies.append(copy)
+        return copies
+
+    query_copies = to_holders(lambda: planes.at[p], query_send, query_recv)
+    fresh_copies = to_holders(lambda: fresh.at[p], fresh_send, fresh_recv)
+
+    def plane(ref, k):
+        return jnp.concatenate([ref[h, k] for h in range(HOLDERS)], axis=0)
+
+    pairs = slots * KV_HEADS
+    member_row = jnp.where(
+        tag_rows[...] == lax.broadcasted_iota(jnp.int32, (pairs, requests), 1).astype(jnp.float32),
+        1.0,
+        0.0,
+    ).astype(jnp.bfloat16)
+    own_head = head_of((pairs, PLANE), 1) == (
+        lax.broadcasted_iota(jnp.int32, (pairs, PLANE), 0) & (KV_HEADS - 1)
+    )
+    slot_rows = leaving[...].reshape(slots * keep, 2 * PLANE)
+    for copy in query_copies:
+        copy.wait_recv()
+
+    spread = []
+    for k in range(REPEAT):
+        q = plane(planes, k)
+        found = jnp.dot(member_row, q, preferred_element_type=jnp.float32)
+        spread.append(jnp.where(own_head, found, 0.0).astype(jnp.bfloat16))
+    scores = SCALE * lax.dot_general(
+        jnp.concatenate(spread, axis=0),
+        slot_rows[:, :PLANE],
+        (((1,), (1,)), ((), ())),
+        preferred_element_type=jnp.float32,
+    )
+    full = (REPEAT * pairs, slots * keep)
+    same = ((lax.broadcasted_iota(jnp.int32, full, 0) >> 3) & (slots - 1)) == (
+        lax.broadcasted_iota(jnp.int32, full, 1) >> 5
+    )
+    scores = jnp.where(same, scores, NEGATIVE)
+    peak = jnp.max(scores, axis=1, keepdims=True)
+    weights = jnp.where(same, jnp.exp(scores - peak), 0.0)
+    total = jnp.sum(weights, axis=1, keepdims=True)
+    mixed = jnp.dot(
+        weights.astype(jnp.bfloat16), slot_rows[:, PLANE:], preferred_element_type=jnp.float32
+    ) / total
+    mixed = mixed.reshape(REPEAT, pairs, PLANE)
+    mixed = jnp.where(own_head[None], mixed, 0.0)
+    mixed = jnp.sum(mixed.reshape(REPEAT * slots, KV_HEADS, PLANE), axis=1)
+    sums[p] = mixed.astype(jnp.bfloat16)
+    lse = peak + jnp.log(total)
+    wide = (REPEAT * pairs, 128)
+    row_id = lax.broadcasted_iota(jnp.int32, wide, 0)
+    at = (row_id >> 6) * KV_HEADS + (row_id & (KV_HEADS - 1))
+    lse = jnp.where(lax.broadcasted_iota(jnp.int32, wide, 1) == at, lse, 0.0)
+    lse = jnp.sum(lse.reshape(REPEAT, slots, KV_HEADS, 128), axis=2)
+    lse = lse[0] + lse[1] + lse[2] + lse[3]
+    peaks[p] = jnp.where(
+        lax.broadcasted_iota(jnp.int32, (slots, 128), 1) == 127, tags[...], lse
+    )
+    peak_copies = to_holders(lambda: peaks.at[p], peak_send, peak_recv)
+    sum_copies = to_holders(lambda: sums.at[p], sum_send, sum_recv)
+
+    for copy in fresh_copies:
+        copy.wait_recv()
+    new_keys = plane(fresh, 0).astype(jnp.float32)
+    new_values = plane(fresh, 1).astype(jnp.float32)
+    own = jnp.zeros((requests, 128), jnp.float32)
+    segment_head = head_of((PLANE, 128), 0)
+    segment_lane = lax.broadcasted_iota(jnp.int32, (PLANE, 128), 1)
+    for k in range(REPEAT):
+        q = plane(planes, k).astype(jnp.float32)
+        segment = jnp.where(segment_lane == segment_head + k * KV_HEADS, 1.0, 0.0)
+        own += split_dot(q * new_keys, segment.astype(jnp.bfloat16))
+    own = own * SCALE
+
+    for copy in peak_copies:
+        copy.wait_recv()
+    every = HOLDERS * slots
+    lse = peaks[...].reshape(every, 128)
+    owner = lse[:, 127:128]
+    where_slot = lax.broadcasted_iota(jnp.int32, (every, every), 0)
+    where_lane = lax.broadcasted_iota(jnp.int32, (every, every), 1)
+    owner_row = jnp.sum(jnp.where(where_slot == where_lane, owner, 0.0), axis=0, keepdims=True)
+    request = lax.broadcasted_iota(jnp.int32, (requests, every), 0).astype(jnp.float32)
+    member = jnp.where(request == owner_row, 1.0, 0.0)
+    request = lax.broadcasted_iota(jnp.int32, (every, requests), 1).astype(jnp.float32)
+    slot_member = jnp.where(request == owner, 1.0, 0.0)
+    top = own
+    for s in range(every):
+        top = jnp.maximum(top, jnp.where(member[:, s : s + 1] > 0.0, lse[s : s + 1], NEGATIVE))
+    factor = jnp.exp(lse - exact_dot(slot_member, top))
+    factor = jnp.where(owner >= 0.0, factor, 0.0)
+    own_weight = jnp.exp(own - top)
+    whole = exact_dot(member, factor) + own_weight
+    slot_whole = exact_dot(slot_member, whole)
+    slot_part = factor / jnp.where(owner >= 0.0, slot_whole, 1.0)
+    own_part = own_weight / whole
+    parts = jnp.concatenate([slot_part, own_part], axis=0)
+
+    for copy in sum_copies:
+        copy.wait_recv()
+    slot_sums = sums[...].astype(jnp.float32).reshape(HOLDERS, REPEAT, slots, PLANE)
+    member = member.astype(jnp.bfloat16)
+    spread_head = head_of((128, PLANE), 1)
+    spread_row = lax.broadcasted_iota(jnp.int32, (128, PLANE), 0)
+    results = []
+    for k in range(REPEAT):
+        expand = jnp.where(spread_row == spread_head + k * KV_HEADS, 1.0, 0.0)
+        shares = split_dot(parts, expand.astype(jnp.bfloat16))
+        weighted = (shares[:every] * slot_sums[:, k].reshape(every, PLANE)).astype(jnp.bfloat16)
+        results.append(
+            jnp.dot(member, weighted, preferred_element_type=jnp.float32)
+            + shares[every:] * new_values
+        )
+    attended[...] = jnp.concatenate(
+        [
+            results[k][:, g * HEAD_DIM : (g + 1) * HEAD_DIM]
+            for g in range(KV_HEADS)
+            for k in range(REPEAT)
+        ],
+        axis=1,
+    ).astype(jnp.bfloat16)
+
+    for copy in page_copies:
+        copy.wait_recv()
+    kept.wait()
+    for copy in (
+        list(moved.values()) + page_copies + proj_copies + query_copies + fresh_copies
+        + peak_copies + sum_copies
+    ):
+        copy.wait_send()
+
+
+def fused_device(
+    tokens, norm_gain, w_query, w_keyvalue, cache, page_count, page_owner, keep_rows, dest_slot
+):
+    slots, _, page_rows, width = cache.shape
+    keep = keep_rows.shape[2]
+    requests, model = tokens.shape
+    part = requests // HOLDERS
+    is_live = jnp.arange(slots) < page_count[0, 0]
+    chosen = (dest_slot[:, 0][None, :] == jnp.arange(slots)[:, None]) & is_live[None, :]
+    code = jnp.where(chosen[:, None, :], keep_rows[:, 0].T[None], -1).reshape(slots * keep, slots)
+    tags = jnp.sum(jnp.where(chosen, page_owner[:, 0][None, :] + 1, 0), axis=1) - 1
+    tags = tags.astype(jnp.float32)
+    vmem = pl.BlockSpec(memory_space=pltpu.VMEM)
+    anywhere = pl.BlockSpec(memory_space=pl.ANY)
+    bf16, f32 = jnp.bfloat16, jnp.float32
+    dma = pltpu.SemaphoreType.DMA
+    attended, compacted = pl.pallas_call(
+        fused_kernel,
+        out_shape=(
+            jax.ShapeDtypeStruct((requests, HEADS * HEAD_DIM), bf16),
+            jax.ShapeDtypeStruct((slots, keep, width), bf16),
+        ),
+        in_specs=[vmem] * 5 + [anywhere] * 3,
+        out_specs=(vmem, anywhere),
+        scratch_shapes=[
+            pltpu.VMEM(w_query.shape, bf16),
+            pltpu.VMEM(w_keyvalue.shape, bf16),
+            pltpu.VMEM((slots * page_rows, width), bf16),
+            pltpu.VMEM((GROUPS, part, model), bf16),
+            pltpu.VMEM((slots, keep, width), bf16),
+            pltpu.VMEM((GROUPS, part, 512), bf16),
+            pltpu.VMEM((GROUPS, part, 512), bf16),
+            pltpu.VMEM((HOLDERS, REPEAT, part, PLANE), bf16),
+            pltpu.VMEM((HOLDERS, 2, part, PLANE), bf16),
+            pltpu.VMEM((HOLDERS, REPEAT * slots, PLANE), bf16),
+            pltpu.VMEM((HOLDERS, slots, 128), f32),
+            dma((3,)),
+            dma,
+            dma((GROUPS,)),
+            dma((GROUPS,)),
+            dma((HOLDERS,)),
+            dma((HOLDERS,)),
+            dma((GROUPS,)),
+            dma((GROUPS,)),
+        ]
+        + [dma((HOLDERS,))] * 8,
+        compiler_params=pltpu.CompilerParams(
+            collective_id=0, has_side_effects=True, vmem_limit_bytes=48 * 1024 * 1024
+        ),
+        cost_estimate=pl.CostEstimate(
+            flops=1_500_000_000, bytes_accessed=7_000_000, transcendentals=70_000
+        ),
+    )(
+        tokens.reshape(HOLDERS, part, model),
+        norm_gain.reshape(1, model),
+        code,
+        tags.reshape(slots, 1),
+        jnp.repeat(tags, KV_HEADS).reshape(slots * KV_HEADS, 1),
+        w_query,
+        w_keyvalue,
+        cache.reshape(slots * page_rows, width),
+    )
+    return attended, compacted[:, None]
+
+
+def local_step(sizes, tokens, norm_gain, w_query, w_keyvalue, cache, *rest):
+    fits = (
+        sizes == {"page": HOLDERS, "tensor": GROUPS}
+        and tokens.shape[0] == 64
+        and cache.shape[0] == 8
+        and rest[2].shape[2] == 32
+    )
+    step = fused_device if fits else per_device
+    return step(tokens, norm_gain, w_query, w_keyvalue, cache, *rest)
+
+
 def solution(mesh):
     return jax.shard_map(
-        per_device,
+        functools.partial(local_step, dict(mesh.shape)),
         mesh=mesh,
         in_specs=(
             P("tensor", None),

time: 170 us -> 47 us (0.28)
  waiting for transfers between devices: 69.7 us -> 0 us
  Pallas kernels: 0 us -> 33.8 us
  blocking collectives: 21.1 us -> 0 us
  local copies, waits for them, and re-layouts: 26.1 us -> 9.35 us
  matrix products: 15.1 us -> 0 us
  between operations: 14.9 us -> 1.33 us
  starting transfers between devices: 11.3 us -> 0 us
  other arithmetic: 11.2 us -> 2.12 us
    all_gather x1 -> x0, waiting for transfers between devices: 38.7 us -> none  [per_device(): portion = lax.all_gather(normed, 'tensor', axis=0, tiled=True)]
    pallas_call x0 -> x1, Pallas kernels: none -> 33.8 us  [fused_device(): pl.pallas_call(fused_kernel, out_shape=(jax.ShapeDtypeStruct((requests, H...]
    psum x1 -> x0, waiting for transfers between devices: 24.2 us -> none  [per_device(): sum_out, sum_total = lax.psum((part_out, part_total), 'page')]
    dot_general x8 -> x0, matrix products: 15.1 us -> none  [the longest x1 3.98 us: per_device(): query_part = jnp.dot(portion, w_query, preferred_element_type=jnp.float32)]
    all_to_all x3 -> x0, starting transfers between devices: 11.2 us -> none  [the longest x1 4.21 us: per_device(): lax.all_to_all(out_tags.reshape(holders, capacity), 'page', split_axis=0,...]
    psum x1 -> x0, blocking collectives: 10.8 us -> none  [per_device(): sum_out, sum_total = lax.psum((part_out, part_total), 'page')]
    pmax x1 -> x0, blocking collectives: 10.3 us -> none  [per_device(): row_peak = jnp.maximum(lax.pmax(local_peak, 'page'), own_score)]
    reshape x7 -> x1, local copies, waits for them, and re-layouts: 9.09 us -> 0.71 us  [fused_device(): norm_gain.reshape(1, model)]
  transfers between devices with their start and end apart: 5 -> 0, of which waited for: 3 -> 0; matrix products, arithmetic and copies ran while one was open for 18% -> 0% of each run, Pallas kernels for 0% -> 0%
where the time goes in v1:
time: 47 us; the launch traced here: 46.6 us
  Pallas kernels  33.8 us (72%)
  local copies, waits for them, and re-layouts  9.35 us (20%)
  other arithmetic  2.12 us (5%)
  between operations  1.33 us (3%)
    pallas_call x1, Pallas kernels, fused_device(): pl.pallas_call(fused_kernel, out_shape=(jax.ShapeDtypeStruct((requests, H...  33.8 us
    unnamed x6, local copies, waits for them, and re-layouts  7.65 us

profile of v1, /device:TPU:0, one launch (start us, length us, event | category | flops | bytes accessed | tf_op | source)
XLA Modules:
  0.0 46.6 jit_solution(14188566239228398851)
XLA Ops:
  1.3 0.7 %add_bitcast_fusion = s32[8]{0:T(128)S(1)} fusion(s32[8,1]{0,1:T(1,128)} %param.15), kind=kLoop, calls=%fused_computation.5 | loop fusion | flops 8 | bytes 64 | tf_op jit(solution)/shard_map/add | solution.py:428
  1.9 0.8 %select_reduce_fusion = s32[8]{0:T(128)S(1)} fusion(s32[8]{0:T(128)S(1)} %add_bitcast_fusion, pred[8]{0:T(512)(128)(4,1)S(1)} %iota_compare_fusion.1, s32[8]{0:T(128)} %bitcast.21), kind=kLoop, calls=%fused_computation.1 | loop fusion | flops 248 | bytes 104 | tf_op jit(solution)/shard_map/reduce_sum | solution.py:428
  2.7 0.7 %fusion = pred[8,8]{1,0:T(8,128)(4,1)S(1)} fusion(s32[8]{0:T(128)} %bitcast.22, pred[8]{0:T(512)(128)(4,1)S(1)} %iota_compare_fusion.1), kind=kLoop, calls=%fused_computation.3 | loop fusion | flops 128 | bytes 104 | tf_op jit(solution)/shard_map/and | solution.py:426
  3.4 0.1 broadcast_in_dim.47
  3.5 0.1 copy.12.tags
  3.5 0.7 %reshape.79.gain = f32[1,2560]{1,0:T(1,128)S(1)} reshape(f32[2560]{0:T(1024)} %param.10) | data formatting | bytes 20480 | tf_op jit(solution)/shard_map/reshape | solution.py:472
  4.3 0.8 %copy.11 = s32[32,8]{1,0:T(8,128)S(1)} copy(s32[32,8]{0,1:T(8,128)} %bitcast.20) | data formatting | bytes 2048 | tf_op jit(solution)/shard_map/transpose | solution.py:427
  5.0 0.1 reshape_reshape.4.tag_rows
  5.1 1.5 %copy.15.w_keyvalue = bf16[2560,160]{1,0:T(8,128)(2,1)S(1)} copy(bf16[2560,160]{0,1:T(8,128)(2,1)} %param.12) | data formatting | bytes 1638400 | tf_op args[3]
  6.6 3.6 %copy.14.w_query = bf16[2560,320]{1,0:T(8,128)(2,1)S(1)} copy(bf16[2560,320]{0,1:T(8,128)(2,1)} %param.11) | data formatting | bytes 3276800 | tf_op args[2]
  10.2 0.0 copy-start
  10.3 1.0 %copy-done = bf16[64,2560]{1,0:T(8,128)(2,1)S(1)} copy-done((bf16[64,2560]{1,0:T(8,128)(2,1)S(1)}, bf16[64,2560]{1,0:T(8,128)(2,1)}, u32[]{:S(2)}) %copy-start) | copy-done | bytes 327704
  11.2 33.8 %shard_map.104 = (bf16[64,2560]{1,0:T(8,128)(2,1)S(1)}, bf16[8,32,1280]{2,1,0:T(8,128)(2,1)S(1)}) custom-call(bf16[4,16,2560]{2,1,0:T(8,128)(2,1)S(1)} %bitcast.18, f32[1,2560]{1,0:T(1,128)S(1)} %reshape.79.gain, s32[256,8]{1,0:T(8,128)S(1)} %bitcast.17, f32[8,1]{1,0:T(8,128)S(1)} %copy.12.tags, f32[64,1]{1,0:T(8,128)S(1)} %reshape_reshape.4.tag_rows, ...), custom_call_target="tpu_custom_call" | custom-call | flops 1500000000 | bytes 7000000 | tf_op jit(solution)/shard_map/pallas_call | solution.py:434
  45.1 0.7 %copy.20 = bf16[64,2560]{1,0:T(8,128)(2,1)} copy(bf16[64,2560]{1,0:T(8,128)(2,1)S(1)} %get-tuple-element.12) | data formatting | bytes 655360
  45.8 0.8 %copy.21 = bf16[8,1,32,1280]{3,2,1,0:T(8,128)(2,1)} copy(bf16[8,1,32,1280]{3,2,1,0:T(8,128)(2,1)S(1)} %bitcast.16) | data formatting | bytes 1310720
  (3 shorter events, 0.0 us)
Async XLA Ops:
  10.2 1.0 %copy-start = (bf16[64,2560]{1,0:T(8,128)(2,1)S(1)}, bf16[64,2560]{1,0:T(8,128)(2,1)}, u32[]{:S(2)}) copy-start(bf16[64,2560]{1,0:T(8,128)(2,1)} %param.9) | copy-start | bytes 983044

commit v2 on v1

--- a/solution.py
+++ b/solution.py
@@ -145,9 +145,9 @@
 
 
 def fused_kernel(
-    tokens, gain, code, tags, tag_rows, w_query, w_keyvalue, cache,
+    tokens, gain, count, owners, targets, kept_rows, w_query, w_keyvalue, cache,
     attended, compacted,
-    wq, wkv, pages, rows, leaving, projected, local, planes, fresh, sums, peaks,
+    weight, pages, rows, leaving, projected, local, planes, fresh, sums, peaks,
     load_sem, keep_sem, row_send, row_recv, page_send, page_recv, proj_send, proj_recv,
     query_send, query_recv, fresh_send, fresh_recv, sum_send, sum_recv, peak_send, peak_recv,
 ):
@@ -155,15 +155,15 @@
     t = lax.axis_index("tensor")
     part = rows.shape[1]
     requests = part * HOLDERS
-    slots = tags.shape[0]
+    slots = leaving.shape[0]
     keep = leaving.shape[1]
     cap = slots // HOLDERS
     page_rows = cache.shape[0] // slots
 
     loads = [
         pltpu.make_async_copy(cache, pages, load_sem.at[0]),
-        pltpu.make_async_copy(w_query, wq, load_sem.at[1]),
-        pltpu.make_async_copy(w_keyvalue, wkv, load_sem.at[2]),
+        pltpu.make_async_copy(w_query, weight.at[pl.ds(0, 320)], load_sem.at[1]),
+        pltpu.make_async_copy(w_keyvalue, weight.at[pl.ds(320, 160)], load_sem.at[2]),
     ]
     for load in loads:
         load.start()
@@ -174,9 +174,12 @@
     for f in range(1, HOLDERS):
         pl.semaphore_signal(barrier, inc=1, device_id=(partner(p, f), t), device_id_type=MESH)
 
+    weight[480:512] = jnp.zeros((32, weight.shape[1]), weight.dtype)
+    gains = gain[...]
+    gains = jnp.concatenate([gains[i : i + 1] for i in range(gains.shape[0])], axis=1)
     mine = tokens[p].astype(jnp.float32)
     square = jnp.mean(mine * mine, axis=-1, keepdims=True)
-    rows[0] = (mine * lax.rsqrt(square + EPSILON) * gain[...]).astype(jnp.bfloat16)
+    rows[0] = (mine * lax.rsqrt(square + EPSILON) * gains).astype(jnp.bfloat16)
     pl.semaphore_wait(barrier, GROUPS + HOLDERS - 2)
 
     def pass_row(e, f):
@@ -193,13 +196,39 @@
 
     moved = {4: pass_row(0, 4), 2: pass_row(0, 2), 1: pass_row(0, 1)}
 
+    live = lax.broadcasted_iota(jnp.int32, (1, slots), 1) < count[...]
+    target = jnp.where(live, targets[...], -1)
+    owner_plus = owners[...].astype(jnp.float32) + 1.0
+
+    def tags_of(shape, shift):
+        at = lax.broadcasted_iota(jnp.int32, shape, 0) >> shift
+        return jnp.sum(jnp.where(target == at, owner_plus, 0.0), axis=1, keepdims=True) - 1.0
+
+    pairs = slots * KV_HEADS
+    tags = tags_of((slots, slots), 0)
+    tag_rows = tags_of((pairs, slots), 3)
+    picks = jnp.concatenate([kept_rows[s] for s in range(slots)], axis=0).astype(jnp.float32)
+    placed = (slots * keep, keep)
+    repeat_rows = jnp.where(
+        (lax.broadcasted_iota(jnp.int32, placed, 0) & (keep - 1))
+        == lax.broadcasted_iota(jnp.int32, placed, 1),
+        1.0,
+        0.0,
+    )
+    code = lax.dot_general(
+        repeat_rows.astype(jnp.bfloat16),
+        picks.astype(jnp.bfloat16),
+        (((1,), (1,)), ((), ())),
+        preferred_element_type=jnp.float32,
+    )
+    at = lax.broadcasted_iota(jnp.int32, (slots * keep, slots), 0) >> 5
+    code = jnp.where(target == at, code, -1.0)
+    lane = lax.broadcasted_iota(jnp.int32, (slots * keep, page_rows), 1).astype(jnp.float32)
+    choice = jnp.concatenate(
+        [jnp.where(code[:, s : s + 1] == lane, 1.0, 0.0).astype(jnp.bfloat16) for s in range(slots)],
+        axis=1,
+    )
     loads[0].wait()
-    lane = lax.broadcasted_iota(jnp.int32, (slots * keep, page_rows), 1)
-    code_values = code[...]
-    choice = jnp.concatenate(
-        [jnp.where(code_values[:, s : s + 1] == lane, 1.0, 0.0).astype(jnp.bfloat16) for s in range(slots)],
-        axis=1,
-    )
     out = jnp.dot(choice, pages[...], preferred_element_type=jnp.float32).astype(jnp.bfloat16)
     leaving[...] = out.reshape(leaving.shape)
     page_copies = []
@@ -231,10 +260,12 @@
 
     def project(first):
         batch = jnp.concatenate([rows[e] for e in range(first, GROUPS, 2)], axis=0)
-        query = jnp.dot(batch, wq[...], preferred_element_type=jnp.float32)
-        pair = jnp.dot(batch, wkv[...], preferred_element_type=jnp.float32)
-        spare = jnp.zeros((batch.shape[0], projected.shape[2] - 480), jnp.float32)
-        both = jnp.concatenate([query, pair, spare], axis=1).astype(jnp.bfloat16)
+        both = lax.dot_general(
+            batch,
+            weight[...],
+            (((1,), (1,)), ((), ())),
+            preferred_element_type=jnp.float32,
+        ).astype(jnp.bfloat16)
         copies = []
         for n, e in enumerate(range(first, GROUPS, 2)):
             block = both[n * part : (n + 1) * part]
@@ -292,9 +323,8 @@
     def plane(ref, k):
         return jnp.concatenate([ref[h, k] for h in range(HOLDERS)], axis=0)
 
-    pairs = slots * KV_HEADS
     member_row = jnp.where(
-        tag_rows[...] == lax.broadcasted_iota(jnp.int32, (pairs, requests), 1).astype(jnp.float32),
+        tag_rows == lax.broadcasted_iota(jnp.int32, (pairs, requests), 1).astype(jnp.float32),
         1.0,
         0.0,
     ).astype(jnp.bfloat16)
@@ -339,7 +369,7 @@
     lse = jnp.sum(lse.reshape(REPEAT, slots, KV_HEADS, 128), axis=2)
     lse = lse[0] + lse[1] + lse[2] + lse[3]
     peaks[p] = jnp.where(
-        lax.broadcasted_iota(jnp.int32, (slots, 128), 1) == 127, tags[...], lse
+        lax.broadcasted_iota(jnp.int32, (slots, 128), 1) == 127, tags, lse
     )
     peak_copies = to_holders(lambda: peaks.at[p], peak_send, peak_recv)
     sum_copies = to_holders(lambda: sums.at[p], sum_send, sum_recv)
@@ -422,11 +452,6 @@
     keep = keep_rows.shape[2]
     requests, model = tokens.shape
     part = requests // HOLDERS
-    is_live = jnp.arange(slots) < page_count[0, 0]
-    chosen = (dest_slot[:, 0][None, :] == jnp.arange(slots)[:, None]) & is_live[None, :]
-    code = jnp.where(chosen[:, None, :], keep_rows[:, 0].T[None], -1).reshape(slots * keep, slots)
-    tags = jnp.sum(jnp.where(chosen, page_owner[:, 0][None, :] + 1, 0), axis=1) - 1
-    tags = tags.astype(jnp.float32)
     vmem = pl.BlockSpec(memory_space=pltpu.VMEM)
     anywhere = pl.BlockSpec(memory_space=pl.ANY)
     bf16, f32 = jnp.bfloat16, jnp.float32
@@ -437,11 +462,10 @@
             jax.ShapeDtypeStruct((requests, HEADS * HEAD_DIM), bf16),
             jax.ShapeDtypeStruct((slots, keep, width), bf16),
         ),
-        in_specs=[vmem] * 5 + [anywhere] * 3,
+        in_specs=[vmem] * 6 + [anywhere] * 3,
         out_specs=(vmem, anywhere),
         scratch_shapes=[
-            pltpu.VMEM(w_query.shape, bf16),
-            pltpu.VMEM(w_keyvalue.shape, bf16),
+            pltpu.VMEM((512, model), bf16),
             pltpu.VMEM((slots * page_rows, width), bf16),
             pltpu.VMEM((GROUPS, part, model), bf16),
             pltpu.VMEM((slots, keep, width), bf16),
@@ -469,12 +493,13 @@
         ),
     )(
         tokens.reshape(HOLDERS, part, model),
-        norm_gain.reshape(1, model),
-        code,
-        tags.reshape(slots, 1),
-        jnp.repeat(tags, KV_HEADS).reshape(slots * KV_HEADS, 1),
-        w_query,
-        w_keyvalue,
+        norm_gain.reshape(model // 128, 128),
+        page_count,
+        page_owner.reshape(1, slots),
+        dest_slot.reshape(1, slots),
+        keep_rows,
+        w_query.T,
+        w_keyvalue.T,
         cache.reshape(slots * page_rows, width),
     )
     return attended, compacted[:, None]

time: 47 us -> 43.5 us (0.926)
  other arithmetic: 2.12 us -> 0 us
  local copies, waits for them, and re-layouts: 9.35 us -> 7.8 us
    reduce_sum x1 -> x0, other arithmetic: 0.77 us -> none  [fused_device(): jnp.sum(jnp.where(chosen, page_owner[:, 0][None, :] + 1, 0), axis=1) - 1]
    transpose x1 -> x0, local copies, waits for them, and re-layouts: 0.76 us -> none  [fused_device(): keep_rows[:, 0].T[None]]
    reshape x1 -> x0, local copies, waits for them, and re-layouts: 0.71 us -> none  [fused_device(): norm_gain.reshape(1, model)]
    and x1 -> x0, other arithmetic: 0.66 us -> none  [fused_device(): (dest_slot[:, 0][None, :] == jnp.arange(slots)[:, None]) & is_live[None, :]]
    add x1 -> x0, other arithmetic: 0.66 us -> none  [fused_device(): page_owner[:, 0][None, :] + 1]
    unnamed x6 -> x16, local copies, waits for them, and re-layouts: 7.65 us -> 7.8 us
where the time goes in v2:
time: 43.5 us; the launch traced here: 43.1 us
  Pallas kernels  34 us (78%)
  local copies, waits for them, and re-layouts  7.8 us (18%)
  between operations  1.3 us (3%)
    pallas_call x1, Pallas kernels, fused_device(): pl.pallas_call(fused_kernel, out_shape=(jax.ShapeDtypeStruct((requests, H...  34 us
    unnamed x16, local copies, waits for them, and re-layouts  7.8 us

profile of v2, /device:TPU:0, one launch (start us, length us, event | category | flops | bytes accessed | tf_op | source)
XLA Modules:
  0.0 43.1 jit_solution(6891451606823245229)
XLA Ops:
  1.3 0.0 copy-start
  1.3 1.4 %copy-done = bf16[2560,320]{0,1:T(8,128)(2,1)S(1)} copy-done((bf16[2560,320]{0,1:T(8,128)(2,1)S(1)}, bf16[2560,320]{0,1:T(8,128)(2,1)}, u32[]{:S(2)}) %copy-start) | copy-done | bytes 1638424
  2.7 0.0 copy-start.1
  2.7 1.1 %copy-done.1 = bf16[2560,160]{0,1:T(8,128)(2,1)S(1)} copy-done((bf16[2560,160]{0,1:T(8,128)(2,1)S(1)}, bf16[2560,160]{0,1:T(8,128)(2,1)}, u32[]{:S(2)}) %copy-start.1) | copy-done | bytes 819224
  3.9 0.0 copy-start.2
  3.9 1.0 %copy-done.2 = bf16[64,2560]{1,0:T(8,128)(2,1)S(1)} copy-done((bf16[64,2560]{1,0:T(8,128)(2,1)S(1)}, bf16[64,2560]{1,0:T(8,128)(2,1)}, u32[]{:S(2)}) %copy-start.2) | copy-done | bytes 327704
  4.8 0.0 copy-start.3
  4.8 0.7 %copy-done.3 = f32[2560]{0:T(1024)S(1)} copy-done((f32[2560]{0:T(1024)S(1)}, f32[2560]{0:T(1024)}, u32[]{:S(2)}) %copy-start.3) | copy-done | bytes 10264
  5.5 0.0 copy-start.4
  5.5 0.7 %copy-done.4 = s32[8,1,32]{2,1,0:T(1,128)S(1)} copy-done((s32[8,1,32]{2,1,0:T(1,128)S(1)}, s32[8,1,32]{2,1,0:T(1,128)}, u32[]{:S(2)}) %copy-start.4) | copy-done | bytes 1048
  6.2 0.0 copy-start.5
  6.2 0.7 %copy-done.5 = s32[8,1]{0,1:T(1,128)S(1)} copy-done((s32[8,1]{0,1:T(1,128)S(1)}, s32[8,1]{0,1:T(1,128)}, u32[]{:S(2)}) %copy-start.5) | copy-done | bytes 56
  6.9 0.0 copy-start.6
  6.9 0.7 %copy-done.6 = s32[8,1]{0,1:T(1,128)S(1)} copy-done((s32[8,1]{0,1:T(1,128)S(1)}, s32[8,1]{0,1:T(1,128)}, u32[]{:S(2)}) %copy-start.6) | copy-done | bytes 56
  7.5 34.0 %shard_map.104 = (bf16[64,2560]{1,0:T(8,128)(2,1)S(1)}, bf16[8,32,1280]{2,1,0:T(8,128)(2,1)S(1)}) custom-call(bf16[4,16,2560]{2,1,0:T(8,128)(2,1)S(1)} %bitcast.13, f32[20,128]{1,0:T(8,128)S(1)} %bitcast.14, s32[1,1]{1,0:T(1,128)S(6)} %copy.14.count, s32[1,8]{1,0:T(1,128)S(1)} %bitcast.15, s32[1,8]{1,0:T(1,128)S(1)} %bitcast.16, s32[8,1,32]{2,1,0:T(1,128)S(1)} %copy-done.4, ...), custom_call_target="tpu_custom_call" | custom-call | flops 1500000000 | bytes 7000000 | tf_op jit(solution)/shard_map/pallas_call | solution.py:459
  41.6 0.7 %copy.15 = bf16[64,2560]{1,0:T(8,128)(2,1)} copy(bf16[64,2560]{1,0:T(8,128)(2,1)S(1)} %get-tuple-element.10) | data formatting | bytes 655360
  42.3 0.8 %copy.16 = bf16[8,1,32,1280]{3,2,1,0:T(8,128)(2,1)} copy(bf16[8,1,32,1280]{3,2,1,0:T(8,128)(2,1)S(1)} %bitcast.10) | data formatting | bytes 1310720
Async XLA Ops:
  1.3 1.4 %copy-start = (bf16[2560,320]{0,1:T(8,128)(2,1)S(1)}, bf16[2560,320]{0,1:T(8,128)(2,1)}, u32[]{:S(2)}) copy-start(bf16[2560,320]{0,1:T(8,128)(2,1)} %param.11) | copy-start | bytes 4915204
  2.7 1.1 %copy-start.1 = (bf16[2560,160]{0,1:T(8,128)(2,1)S(1)}, bf16[2560,160]{0,1:T(8,128)(2,1)}, u32[]{:S(2)}) copy-start(bf16[2560,160]{0,1:T(8,128)(2,1)} %param.12) | copy-start | bytes 2457604
  3.9 1.0 %copy-start.2 = (bf16[64,2560]{1,0:T(8,128)(2,1)S(1)}, bf16[64,2560]{1,0:T(8,128)(2,1)}, u32[]{:S(2)}) copy-start(bf16[64,2560]{1,0:T(8,128)(2,1)} %param.9) | copy-start | bytes 983044
  4.8 0.7 %copy-start.3 = (f32[2560]{0:T(1024)S(1)}, f32[2560]{0:T(1024)}, u32[]{:S(2)}) copy-start(f32[2560]{0:T(1024)} %param.10) | copy-start | bytes 30724
  5.5 0.7 %copy-start.4 = (s32[8,1,32]{2,1,0:T(1,128)S(1)}, s32[8,1,32]{2,1,0:T(1,128)}, u32[]{:S(2)}) copy-start(s32[8,1,32]{2,1,0:T(1,128)} %kept_rows.1) | copy-start | bytes 3076
  6.2 0.7 %copy-start.5 = (s32[8,1]{0,1:T(1,128)S(1)}, s32[8,1]{0,1:T(1,128)}, u32[]{:S(2)}) copy-start(s32[8,1]{0,1:T(1,128)} %param.15) | copy-start | bytes 100
  6.9 0.7 %copy-start.6 = (s32[8,1]{0,1:T(1,128)S(1)}, s32[8,1]{0,1:T(1,128)}, u32[]{:S(2)}) copy-start(s32[8,1]{0,1:T(1,128)} %param.17) | copy-start | bytes 100

commit v3 on v2

--- a/solution.py
+++ b/solution.py
@@ -145,15 +145,15 @@
 
 
 def fused_kernel(
-    tokens, gain, count, owners, targets, kept_rows, w_query, w_keyvalue, cache,
+    tokens_in, gain_in, count_in, owners_in, targets_in, kept_in, w_query, w_keyvalue, cache,
     attended, compacted,
-    weight, pages, rows, leaving, projected, local, planes, fresh, sums, peaks,
+    tokens, gain, count, owners, targets, kept_rows, weight, pages, rows, leaving, projected, local, planes, fresh, sums, peaks,
     load_sem, keep_sem, row_send, row_recv, page_send, page_recv, proj_send, proj_recv,
     query_send, query_recv, fresh_send, fresh_recv, sum_send, sum_recv, peak_send, peak_recv,
 ):
     p = lax.axis_index("page")
     t = lax.axis_index("tensor")
-    part = rows.shape[1]
+    part = rows.shape[2]
     requests = part * HOLDERS
     slots = leaving.shape[0]
     keep = leaving.shape[1]
@@ -161,6 +161,12 @@
     page_rows = cache.shape[0] // slots
 
     loads = [
+        pltpu.make_async_copy(tokens_in.at[p], tokens, load_sem.at[3]),
+        pltpu.make_async_copy(gain_in, gain, load_sem.at[4]),
+        pltpu.make_async_copy(count_in, count, load_sem.at[5]),
+        pltpu.make_async_copy(owners_in, owners, load_sem.at[6]),
+        pltpu.make_async_copy(targets_in, targets, load_sem.at[7]),
+        pltpu.make_async_copy(kept_in, kept_rows, load_sem.at[8]),
         pltpu.make_async_copy(cache, pages, load_sem.at[0]),
         pltpu.make_async_copy(w_query, weight.at[pl.ds(0, 320)], load_sem.at[1]),
         pltpu.make_async_copy(w_keyvalue, weight.at[pl.ds(320, 160)], load_sem.at[2]),
@@ -175,27 +181,43 @@
         pl.semaphore_signal(barrier, inc=1, device_id=(partner(p, f), t), device_id_type=MESH)
 
     weight[480:512] = jnp.zeros((32, weight.shape[1]), weight.dtype)
+    loads[0].wait()
+    loads[1].wait()
     gains = gain[...]
     gains = jnp.concatenate([gains[i : i + 1] for i in range(gains.shape[0])], axis=1)
-    mine = tokens[p].astype(jnp.float32)
+    mine = tokens[...].astype(jnp.float32)
     square = jnp.mean(mine * mine, axis=-1, keepdims=True)
-    rows[0] = (mine * lax.rsqrt(square + EPSILON) * gains).astype(jnp.bfloat16)
+    normed = (mine * lax.rsqrt(square + EPSILON) * gains).astype(jnp.bfloat16)
+    half = normed.shape[1] // 2
+    rows[0, 0] = normed[:, :half]
+    rows[1, 0] = normed[:, half:]
     pl.semaphore_wait(barrier, GROUPS + HOLDERS - 2)
 
-    def pass_row(e, f):
+    def pass_row(h, e, f):
         copy = pltpu.make_async_remote_copy(
-            src_ref=rows.at[e],
-            dst_ref=rows.at[e ^ f],
-            send_sem=row_send.at[e ^ f],
-            recv_sem=row_recv.at[e ^ f],
+            src_ref=rows.at[h, e],
+            dst_ref=rows.at[h, e ^ f],
+            send_sem=row_send.at[h, e ^ f],
+            recv_sem=row_recv.at[h, e ^ f],
             device_id=(p, partner(t, f)),
             device_id_type=MESH,
         )
         copy.start()
         return copy
 
-    moved = {4: pass_row(0, 4), 2: pass_row(0, 2), 1: pass_row(0, 1)}
-
+    moved = {}
+    for h in range(2):
+        for f in (4, 2, 1):
+            moved[h, f] = pass_row(h, 0, f)
+
+    def forward(h, e):
+        moved[h, e].wait_recv()
+        if e == 4:
+            moved[h, 6] = pass_row(h, 4, 2)
+        moved[h, e + 1] = pass_row(h, e, 1)
+
+    for load in loads[2:6]:
+        load.wait()
     live = lax.broadcasted_iota(jnp.int32, (1, slots), 1) < count[...]
     target = jnp.where(live, targets[...], -1)
     owner_plus = owners[...].astype(jnp.float32) + 1.0
@@ -228,8 +250,14 @@
         [jnp.where(code[:, s : s + 1] == lane, 1.0, 0.0).astype(jnp.bfloat16) for s in range(slots)],
         axis=1,
     )
-    loads[0].wait()
-    out = jnp.dot(choice, pages[...], preferred_element_type=jnp.float32).astype(jnp.bfloat16)
+    loads[6].wait()
+    forward(0, 4)
+    forward(0, 2)
+    left = jnp.dot(choice, pages[:, :PLANE], preferred_element_type=jnp.float32)
+    forward(1, 4)
+    forward(1, 2)
+    right = jnp.dot(choice, pages[:, PLANE:], preferred_element_type=jnp.float32)
+    out = jnp.concatenate([left, right], axis=1).astype(jnp.bfloat16)
     leaving[...] = out.reshape(leaving.shape)
     page_copies = []
     for f in range(1, HOLDERS):
@@ -248,24 +276,24 @@
     )
     kept.start()
 
-    moved[4].wait_recv()
-    moved[6] = pass_row(4, 2)
-    moved[5] = pass_row(4, 1)
-    moved[2].wait_recv()
-    moved[3] = pass_row(2, 1)
-    loads[1].wait()
-    loads[2].wait()
-    moved[6].wait_recv()
-    moved[7] = pass_row(6, 1)
+    loads[7].wait()
+    loads[8].wait()
+    forward(0, 6)
+    forward(1, 6)
 
     def project(first):
-        batch = jnp.concatenate([rows[e] for e in range(first, GROUPS, 2)], axis=0)
-        both = lax.dot_general(
-            batch,
-            weight[...],
-            (((1,), (1,)), ((), ())),
-            preferred_element_type=jnp.float32,
-        ).astype(jnp.bfloat16)
+        both = 0.0
+        for h in range(2):
+            if first == 1:
+                for e in (1, 3, 5, 7):
+                    moved[h, e].wait_recv()
+            both += lax.dot_general(
+                jnp.concatenate([rows[h, e] for e in range(first, GROUPS, 2)], axis=0),
+                weight[:, h * half : (h + 1) * half],
+                (((1,), (1,)), ((), ())),
+                preferred_element_type=jnp.float32,
+            )
+        both = both.astype(jnp.bfloat16)
         copies = []
         for n, e in enumerate(range(first, GROUPS, 2)):
             block = both[n * part : (n + 1) * part]
@@ -286,8 +314,6 @@
         return copies
 
     proj_copies = project(0)
-    for e in (1, 3, 5, 7):
-        moved[e].wait_recv()
     proj_copies += project(1)
     for copy in proj_copies:
         copy.wait_recv()
@@ -462,12 +488,18 @@
             jax.ShapeDtypeStruct((requests, HEADS * HEAD_DIM), bf16),
             jax.ShapeDtypeStruct((slots, keep, width), bf16),
         ),
-        in_specs=[vmem] * 6 + [anywhere] * 3,
+        in_specs=[anywhere] * 9,
         out_specs=(vmem, anywhere),
         scratch_shapes=[
+            pltpu.VMEM((part, model), bf16),
+            pltpu.VMEM((model // 128, 128), f32),
+            pltpu.VMEM((1, 1), jnp.int32),
+            pltpu.VMEM((1, slots), jnp.int32),
+            pltpu.VMEM((1, slots), jnp.int32),
+            pltpu.VMEM(keep_rows.shape, jnp.int32),
             pltpu.VMEM((512, model), bf16),
             pltpu.VMEM((slots * page_rows, width), bf16),
-            pltpu.VMEM((GROUPS, part, model), bf16),
+            pltpu.VMEM((2, GROUPS, part, model // 2), bf16),
             pltpu.VMEM((slots, keep, width), bf16),
             pltpu.VMEM((GROUPS, part, 512), bf16),
             pltpu.VMEM((GROUPS, part, 512), bf16),
@@ -475,10 +507,10 @@
             pltpu.VMEM((HOLDERS, 2, part, PLANE), bf16),
             pltpu.VMEM((HOLDERS, REPEAT * slots, PLANE), bf16),
             pltpu.VMEM((HOLDERS, slots, 128), f32),
-            dma((3,)),
+            dma((9,)),
             dma,
-            dma((GROUPS,)),
-            dma((GROUPS,)),
+            dma((2, GROUPS)),
+            dma((2, GROUPS)),
             dma((HOLDERS,)),
             dma((HOLDERS,)),
             dma((GROUPS,)),
@@ -486,7 +518,7 @@
         ]
         + [dma((HOLDERS,))] * 8,
         compiler_params=pltpu.CompilerParams(
-            collective_id=0, has_side_effects=True, vmem_limit_bytes=48 * 1024 * 1024
+            collective_id=0, has_side_effects=True, vmem_limit_bytes=60 * 1024 * 1024
         ),
         cost_estimate=pl.CostEstimate(
             flops=1_500_000_000, bytes_accessed=7_000_000, transcendentals=70_000

time: 43.5 us -> 40 us (0.920)
  local copies, waits for them, and re-layouts: 7.8 us -> 3.68 us
  Pallas kernels: 34 us -> 34.9 us
    unnamed x16 -> x2, local copies, waits for them, and re-layouts: 7.8 us -> 3.68 us
    pallas_call x1, Pallas kernels: 34 us -> 34.9 us  [fused_device(): pl.pallas_call(fused_kernel, out_shape=(jax.ShapeDtypeStruct((requests, H...]
where the time goes in v3:
time: 40 us; the launch traced here: 39.8 us
  Pallas kernels  34.9 us (87%)
  local copies, waits for them, and re-layouts  3.68 us (9%)
  between operations  1.29 us (3%)
    pallas_call x1, Pallas kernels, fused_device(): pl.pallas_call(fused_kernel, out_shape=(jax.ShapeDtypeStruct((requests, H...  34.9 us
    unnamed x2, local copies, waits for them, and re-layouts  3.68 us

profile of v3, /device:TPU:0, one launch (start us, length us, event | category | flops | bytes accessed | tf_op | source)
XLA Modules:
  0.0 39.8 jit_solution(10335574592106370769)
XLA Ops:
  1.3 34.9 %shard_map.104 = (bf16[64,2560]{1,0:T(8,128)(2,1)}, bf16[8,32,1280]{2,1,0:T(8,128)(2,1)}) custom-call(bf16[4,16,2560]{2,1,0:T(8,128)(2,1)} %bitcast.14, f32[20,128]{1,0:T(8,128)} %bitcast.15, s32[1,1]{1,0:T(1,128)S(6)} %copy.14.count_in, s32[1,8]{1,0:T(1,128)} %bitcast.16, s32[1,8]{1,0:T(1,128)} %bitcast.17, s32[8,1,32]{2,1,0:T(1,128)} %kept_in.1, ...), custom_call_target="tpu_custom_call" | custom-call | flops 1500000000 | bytes 7000000 | tf_op jit(solution)/shard_map/pallas_call | solution.py:485
  36.1 1.7 %copy.15 = bf16[64,2560]{1,0:T(8,128)(2,1)} copy(bf16[64,2560]{1,0:T(8,128)(2,1)} %get-tuple-element.10) | data formatting | bytes 655360
  37.9 2.0 %copy.16 = bf16[8,1,32,1280]{3,2,1,0:T(8,128)(2,1)} copy(bf16[8,1,32,1280]{3,2,1,0:T(8,128)(2,1)} %bitcast.10) | data formatting | bytes 1310720

commit v4 on v3

--- a/solution.py
+++ b/solution.py
@@ -214,7 +214,10 @@
         moved[h, e].wait_recv()
         if e == 4:
             moved[h, 6] = pass_row(h, 4, 2)
-        moved[h, e + 1] = pass_row(h, e, 1)
+        if (h, e) == (1, 5):
+            moved[h, 7] = pass_row(h, 5, 2)
+        elif (h, e) != (1, 6):
+            moved[h, e + 1] = pass_row(h, e, 1)
 
     for load in loads[2:6]:
         load.wait()
@@ -279,6 +282,7 @@
     loads[7].wait()
     loads[8].wait()
     forward(0, 6)
+    forward(1, 5)
     forward(1, 6)
 
     def project(first):
@@ -286,7 +290,8 @@
         for h in range(2):
             if first == 1:
                 for e in (1, 3, 5, 7):
-                    moved[h, e].wait_recv()
+                    if (h, e) != (1, 5):
+                        moved[h, e].wait_recv()
             both += lax.dot_general(
                 jnp.concatenate([rows[h, e] for e in range(first, GROUPS, 2)], axis=0),
                 weight[:, h * half : (h + 1) * half],
@@ -382,11 +387,18 @@
     total = jnp.sum(weights, axis=1, keepdims=True)
     mixed = jnp.dot(
         weights.astype(jnp.bfloat16), slot_rows[:, PLANE:], preferred_element_type=jnp.float32
-    ) / total
+    ) * (1.0 / total)
     mixed = mixed.reshape(REPEAT, pairs, PLANE)
-    mixed = jnp.where(own_head[None], mixed, 0.0)
-    mixed = jnp.sum(mixed.reshape(REPEAT * slots, KV_HEADS, PLANE), axis=1)
-    sums[p] = mixed.astype(jnp.bfloat16)
+    mixed = jnp.where(own_head[None], mixed, 0.0).astype(jnp.bfloat16)
+    gather = (REPEAT * slots, REPEAT * pairs)
+    of_slot = lax.broadcasted_iota(jnp.int32, gather, 0) == (
+        lax.broadcasted_iota(jnp.int32, gather, 1) >> 3
+    )
+    sums[p] = jnp.dot(
+        jnp.where(of_slot, 1.0, 0.0).astype(jnp.bfloat16),
+        mixed.reshape(REPEAT * pairs, PLANE),
+        preferred_element_type=jnp.float32,
+    ).astype(jnp.bfloat16)
     lse = peak + jnp.log(total)
     wide = (REPEAT * pairs, 128)
     row_id = lax.broadcasted_iota(jnp.int32, wide, 0)
@@ -479,7 +491,7 @@
     requests, model = tokens.shape
     part = requests // HOLDERS
     vmem = pl.BlockSpec(memory_space=pltpu.VMEM)
-    anywhere = pl.BlockSpec(memory_space=pl.ANY)
+    pinned = pl.BlockSpec(memory_space=pltpu.HBM)
     bf16, f32 = jnp.bfloat16, jnp.float32
     dma = pltpu.SemaphoreType.DMA
     attended, compacted = pl.pallas_call(
@@ -488,8 +500,8 @@
             jax.ShapeDtypeStruct((requests, HEADS * HEAD_DIM), bf16),
             jax.ShapeDtypeStruct((slots, keep, width), bf16),
         ),
-        in_specs=[anywhere] * 9,
-        out_specs=(vmem, anywhere),
+        in_specs=[pinned] * 9,
+        out_specs=(vmem, vmem),
         scratch_shapes=[
             pltpu.VMEM((part, model), bf16),
             pltpu.VMEM((model // 128, 128), f32),
@@ -518,7 +530,7 @@
         ]
         + [dma((HOLDERS,))] * 8,
         compiler_params=pltpu.CompilerParams(
-            collective_id=0, has_side_effects=True, vmem_limit_bytes=60 * 1024 * 1024
+            collective_id=0, has_side_effects=True, vmem_limit_bytes=48 * 1024 * 1024
         ),
         cost_estimate=pl.CostEstimate(
             flops=1_500_000_000, bytes_accessed=7_000_000, transcendentals=70_000

time: 40 us -> 43.8 us (1.095)
  local copies, waits for them, and re-layouts: 3.68 us -> 7.8 us
  Pallas kernels: 34.9 us -> 34.4 us
    unnamed x2 -> x16, local copies, waits for them, and re-layouts: 3.68 us -> 7.8 us
    pallas_call x1, Pallas kernels: 34.9 us -> 34.4 us  [fused_device(): pl.pallas_call(fused_kernel, out_shape=(jax.ShapeDtypeStruct((requests, H...]
where the time goes in v4:
time: 43.8 us; the launch traced here: 43.5 us
  Pallas kernels  34.4 us (79%)
  local copies, waits for them, and re-layouts  7.8 us (18%)
  between operations  1.3 us (3%)
    pallas_call x1, Pallas kernels, fused_device(): pl.pallas_call(fused_kernel, out_shape=(jax.ShapeDtypeStruct((requests, H...  34.4 us
    unnamed x16, local copies, waits for them, and re-layouts  7.8 us

profile of v4, /device:TPU:0, one launch (start us, length us, event | category | flops | bytes accessed | tf_op | source)
XLA Modules:
  0.0 43.5 jit_solution(13775512880552870538)
XLA Ops:
  1.3 0.0 copy-start
  1.3 1.4 %copy-done = bf16[2560,320]{0,1:T(8,128)(2,1)S(1)} copy-done((bf16[2560,320]{0,1:T(8,128)(2,1)S(1)}, bf16[2560,320]{0,1:T(8,128)(2,1)}, u32[]{:S(2)}) %copy-start) | copy-done | bytes 1638424
  2.7 0.0 copy-start.1
  2.7 1.1 %copy-done.1 = bf16[2560,160]{0,1:T(8,128)(2,1)S(1)} copy-done((bf16[2560,160]{0,1:T(8,128)(2,1)S(1)}, bf16[2560,160]{0,1:T(8,128)(2,1)}, u32[]{:S(2)}) %copy-start.1) | copy-done | bytes 819224
  3.9 0.0 copy-start.2
  3.9 1.0 %copy-done.2 = bf16[64,2560]{1,0:T(8,128)(2,1)S(1)} copy-done((bf16[64,2560]{1,0:T(8,128)(2,1)S(1)}, bf16[64,2560]{1,0:T(8,128)(2,1)}, u32[]{:S(2)}) %copy-start.2) | copy-done | bytes 327704
  4.8 0.0 copy-start.3
  4.8 0.7 %copy-done.3 = f32[2560]{0:T(1024)S(1)} copy-done((f32[2560]{0:T(1024)S(1)}, f32[2560]{0:T(1024)}, u32[]{:S(2)}) %copy-start.3) | copy-done | bytes 10264
  5.5 0.0 copy-start.4
  5.5 0.7 %copy-done.4 = s32[8,1,32]{2,1,0:T(1,128)S(1)} copy-done((s32[8,1,32]{2,1,0:T(1,128)S(1)}, s32[8,1,32]{2,1,0:T(1,128)}, u32[]{:S(2)}) %copy-start.4) | copy-done | bytes 1048
  6.2 0.0 copy-start.5
  6.2 0.7 %copy-done.5 = s32[8,1]{0,1:T(1,128)S(1)} copy-done((s32[8,1]{0,1:T(1,128)S(1)}, s32[8,1]{0,1:T(1,128)}, u32[]{:S(2)}) %copy-start.5) | copy-done | bytes 56
  6.9 0.0 copy-start.6
  6.9 0.7 %copy-done.6 = s32[8,1]{0,1:T(1,128)S(1)} copy-done((s32[8,1]{0,1:T(1,128)S(1)}, s32[8,1]{0,1:T(1,128)}, u32[]{:S(2)}) %copy-start.6) | copy-done | bytes 56
  7.5 34.4 %shard_map.104 = (bf16[64,2560]{1,0:T(8,128)(2,1)S(1)}, bf16[8,32,1280]{2,1,0:T(8,128)(2,1)S(1)}) custom-call(bf16[4,16,2560]{2,1,0:T(8,128)(2,1)S(1)} %bitcast.13, f32[20,128]{1,0:T(8,128)S(1)} %bitcast.14, s32[1,1]{1,0:T(1,128)S(6)} %copy.14.count_in, s32[1,8]{1,0:T(1,128)S(1)} %bitcast.15, s32[1,8]{1,0:T(1,128)S(1)} %bitcast.16, ...), custom_call_target="tpu_custom_call" | custom-call | flops 1500000000 | bytes 7000000 | tf_op jit(solution)/shard_map/pallas_call | solution.py:497
  41.9 0.7 %copy.15 = bf16[64,2560]{1,0:T(8,128)(2,1)} copy(bf16[64,2560]{1,0:T(8,128)(2,1)S(1)} %get-tuple-element.10) | data formatting | bytes 655360
  42.7 0.8 %copy.16 = bf16[8,1,32,1280]{3,2,1,0:T(8,128)(2,1)} copy(bf16[8,1,32,1280]{3,2,1,0:T(8,128)(2,1)S(1)} %bitcast.10) | data formatting | bytes 1310720
Async XLA Ops:
  1.3 1.4 %copy-start = (bf16[2560,320]{0,1:T(8,128)(2,1)S(1)}, bf16[2560,320]{0,1:T(8,128)(2,1)}, u32[]{:S(2)}) copy-start(bf16[2560,320]{0,1:T(8,128)(2,1)} %param.11) | copy-start | bytes 4915204
  2.7 1.1 %copy-start.1 = (bf16[2560,160]{0,1:T(8,128)(2,1)S(1)}, bf16[2560,160]{0,1:T(8,128)(2,1)}, u32[]{:S(2)}) copy-start(bf16[2560,160]{0,1:T(8,128)(2,1)} %param.12) | copy-start | bytes 2457604
  3.9 1.0 %copy-start.2 = (bf16[64,2560]{1,0:T(8,128)(2,1)S(1)}, bf16[64,2560]{1,0:T(8,128)(2,1)}, u32[]{:S(2)}) copy-start(bf16[64,2560]{1,0:T(8,128)(2,1)} %param.9) | copy-start | bytes 983044
  4.8 0.7 %copy-start.3 = (f32[2560]{0:T(1024)S(1)}, f32[2560]{0:T(1024)}, u32[]{:S(2)}) copy-start(f32[2560]{0:T(1024)} %param.10) | copy-start | bytes 30724
  5.5 0.7 %copy-start.4 = (s32[8,1,32]{2,1,0:T(1,128)S(1)}, s32[8,1,32]{2,1,0:T(1,128)}, u32[]{:S(2)}) copy-start(s32[8,1,32]{2,1,0:T(1,128)} %kept_in.1) | copy-start | bytes 3076
  6.2 0.7 %copy-start.5 = (s32[8,1]{0,1:T(1,128)S(1)}, s32[8,1]{0,1:T(1,128)}, u32[]{:S(2)}) copy-start(s32[8,1]{0,1:T(1,128)} %param.15) | copy-start | bytes 100
  6.9 0.7 %copy-start.6 = (s32[8,1]{0,1:T(1,128)S(1)}, s32[8,1]{0,1:T(1,128)}, u32[]{:S(2)}) copy-start(s32[8,1]{0,1:T(1,128)} %param.17) | copy-start | bytes 100

commit v5 on v4

--- a/solution.py
+++ b/solution.py
@@ -481,6 +481,21 @@
         + peak_copies + sum_copies
     ):
         copy.wait_send()
+
+
+def deliver_kernel(attended, compacted, attended_out, compacted_out, sems):
+    copies = []
+    for source, target, pieces in ((attended, attended_out, 2), (compacted, compacted_out, 4)):
+        size = source.shape[0] // pieces
+        for n in range(pieces):
+            piece = pl.ds(n * size, size)
+            copies.append(
+                pltpu.make_async_copy(source.at[piece], target.at[piece], sems.at[len(copies)])
+            )
+    for copy in copies:
+        copy.start()
+    for copy in copies:
+        copy.wait()
 
 
 def fused_device(
@@ -530,7 +545,7 @@
         ]
         + [dma((HOLDERS,))] * 8,
         compiler_params=pltpu.CompilerParams(
-            collective_id=0, has_side_effects=True, vmem_limit_bytes=48 * 1024 * 1024
+            collective_id=0, has_side_effects=True, vmem_limit_bytes=60 * 1024 * 1024
         ),
         cost_estimate=pl.CostEstimate(
             flops=1_500_000_000, bytes_accessed=7_000_000, transcendentals=70_000
@@ -546,6 +561,18 @@
         w_keyvalue.T,
         cache.reshape(slots * page_rows, width),
     )
+    attended, compacted = pl.pallas_call(
+        deliver_kernel,
+        out_shape=(
+            jax.ShapeDtypeStruct(attended.shape, bf16),
+            jax.ShapeDtypeStruct(compacted.shape, bf16),
+        ),
+        in_specs=[pinned] * 2,
+        out_specs=(pinned, pinned),
+        scratch_shapes=[dma((6,))],
+        compiler_params=pltpu.CompilerParams(vmem_limit_bytes=60 * 1024 * 1024),
+        cost_estimate=pl.CostEstimate(flops=0, bytes_accessed=1_966_080, transcendentals=0),
+    )(attended, compacted)
     return attended, compacted[:, None]
 
 

time: 43.8 us -> 67.4 us (1.54)
  Pallas kernels: 34.4 us -> 65.9 us
  local copies, waits for them, and re-layouts: 7.8 us -> 0 us
    pallas_call x0 -> x1, Pallas kernels: none -> 30.9 us  [fused_device(): pl.pallas_call(deliver_kernel, out_shape=(jax.ShapeDtypeStruct(attended.s...]
    unnamed x16 -> x0, local copies, waits for them, and re-layouts: 7.8 us -> none
where the time goes in v5:
time: 67.4 us; the launch traced here: 67.2 us
  Pallas kernels  65.9 us (98%)
  between operations  1.29 us (2%)
    pallas_call x1, Pallas kernels, fused_device(): pl.pallas_call(fused_kernel, out_shape=(jax.ShapeDtypeStruct((requests, H...  35 us
    pallas_call x1, Pallas kernels, fused_device(): pl.pallas_call(deliver_kernel, out_shape=(jax.ShapeDtypeStruct(attended.s...  30.9 us

profile of v5, /device:TPU:0, one launch (start us, length us, event | category | flops | bytes accessed | tf_op | source)
XLA Modules:
  0.0 67.2 jit_solution(1284521923076991738)
XLA Ops:
  1.3 35.0 %shard_map.104 = (bf16[64,2560]{1,0:T(8,128)(2,1)}, bf16[8,32,1280]{2,1,0:T(8,128)(2,1)}) custom-call(bf16[4,16,2560]{2,1,0:T(8,128)(2,1)} %bitcast.14, f32[20,128]{1,0:T(8,128)} %bitcast.15, s32[1,1]{1,0:T(1,128)S(6)} %copy.12.count_in, s32[1,8]{1,0:T(1,128)} %bitcast.16, s32[1,8]{1,0:T(1,128)} %bitcast.17, s32[8,1,32]{2,1,0:T(1,128)} %kept_in.1, ...), custom_call_target="tpu_custom_call" | custom-call | flops 1500000000 | bytes 7000000 | tf_op jit(solution)/shard_map/pallas_call | solution.py:512
  36.3 30.9 %shard_map.105 = (bf16[64,2560]{1,0:T(8,128)(2,1)}, bf16[8,32,1280]{2,1,0:T(8,128)(2,1)}) custom-call(bf16[64,2560]{1,0:T(8,128)(2,1)} %get-tuple-element.6.attended, bf16[8,32,1280]{2,1,0:T(8,128)(2,1)} %get-tuple-element.7.compacted), custom_call_target="tpu_custom_call" | custom-call | bytes 1966080 | tf_op jit(solution)/shard_map/pallas_call | solution.py:564

commit v6 on v5

--- a/solution.py
+++ b/solution.py
@@ -483,16 +483,20 @@
         copy.wait_send()
 
 
-def deliver_kernel(attended, compacted, attended_out, compacted_out, sems):
-    copies = []
-    for source, target, pieces in ((attended, attended_out, 2), (compacted, compacted_out, 4)):
+def deliver_kernel(attended, compacted, attended_out, compacted_out, rows, pages, get, put):
+    fetches, copies = [], []
+    ways = ((attended, rows, attended_out, 2), (compacted, pages, compacted_out, 4))
+    for source, middle, target, pieces in ways:
         size = source.shape[0] // pieces
         for n in range(pieces):
             piece = pl.ds(n * size, size)
-            copies.append(
-                pltpu.make_async_copy(source.at[piece], target.at[piece], sems.at[len(copies)])
-            )
-    for copy in copies:
+            at = len(copies)
+            fetches.append(pltpu.make_async_copy(source.at[piece], middle.at[piece], get.at[at]))
+            copies.append(pltpu.make_async_copy(middle.at[piece], target.at[piece], put.at[at]))
+    for fetch in fetches:
+        fetch.start()
+    for fetch, copy in zip(fetches, copies):
+        fetch.wait()
         copy.start()
     for copy in copies:
         copy.wait()
@@ -569,7 +573,12 @@
         ),
         in_specs=[pinned] * 2,
         out_specs=(pinned, pinned),
-        scratch_shapes=[dma((6,))],
+        scratch_shapes=[
+            pltpu.VMEM(attended.shape, bf16),
+            pltpu.VMEM(compacted.shape, bf16),
+            dma((6,)),
+            dma((6,)),
+        ],
         compiler_params=pltpu.CompilerParams(vmem_limit_bytes=60 * 1024 * 1024),
         cost_estimate=pl.CostEstimate(flops=0, bytes_accessed=1_966_080, transcendentals=0),
     )(attended, compacted)

time: 67.4 us -> 38.5 us (0.57)
  Pallas kernels: 65.9 us -> 37.1 us
    pallas_call x1, Pallas kernels: 30.9 us -> 2.06 us  [fused_device(): pl.pallas_call(deliver_kernel, out_shape=(jax.ShapeDtypeStruct(attended.s...]
where the time goes in v6:
time: 38.5 us; the launch traced here: 38.4 us
  Pallas kernels  37.1 us (96%)
  between operations  1.29 us (3%)
    pallas_call x1, Pallas kernels, fused_device(): pl.pallas_call(fused_kernel, out_shape=(jax.ShapeDtypeStruct((requests, H...  35 us
    pallas_call x1, Pallas kernels, fused_device(): pl.pallas_call(deliver_kernel, out_shape=(jax.ShapeDtypeStruct(attended.s...  2.06 us

profile of v6, /device:TPU:0, one launch (start us, length us, event | category | flops | bytes accessed | tf_op | source)
XLA Modules:
  0.0 38.4 jit_solution(13192565182660305037)
XLA Ops:
  1.3 35.0 %shard_map.104 = (bf16[64,2560]{1,0:T(8,128)(2,1)}, bf16[8,32,1280]{2,1,0:T(8,128)(2,1)}) custom-call(bf16[4,16,2560]{2,1,0:T(8,128)(2,1)} %bitcast.14, f32[20,128]{1,0:T(8,128)} %bitcast.15, s32[1,1]{1,0:T(1,128)S(6)} %copy.12.count_in, s32[1,8]{1,0:T(1,128)} %bitcast.16, s32[1,8]{1,0:T(1,128)} %bitcast.17, s32[8,1,32]{2,1,0:T(1,128)} %kept_in.1, ...), custom_call_target="tpu_custom_call" | custom-call | flops 1500000000 | bytes 7000000 | tf_op jit(solution)/shard_map/pallas_call | solution.py:516
  36.3 2.1 %shard_map.105 = (bf16[64,2560]{1,0:T(8,128)(2,1)}, bf16[8,32,1280]{2,1,0:T(8,128)(2,1)}) custom-call(bf16[64,2560]{1,0:T(8,128)(2,1)} %get-tuple-element.6.attended, bf16[8,32,1280]{2,1,0:T(8,128)(2,1)} %get-tuple-element.7.compacted), custom_call_target="tpu_custom_call" | custom-call | bytes 1966080 | tf_op jit(solution)/shard_map/pallas_call | solution.py:568

commit v7 on v6

--- a/solution.py
+++ b/solution.py
@@ -333,9 +333,9 @@
             [b[:, 320:480] for b in blocks[4 * n : 4 * n + 4]], axis=1
         ).astype(jnp.bfloat16)
 
-    def to_holders(ref_of, send, recv):
+    def to_holders(ref_of, send, recv, flips=(1, 2, 3)):
         copies = []
-        for f in range(1, HOLDERS):
+        for f in flips:
             copy = pltpu.make_async_remote_copy(
                 src_ref=ref_of(),
                 dst_ref=ref_of(),
@@ -348,7 +348,7 @@
             copies.append(copy)
         return copies
 
-    query_copies = to_holders(lambda: planes.at[p], query_send, query_recv)
+    query_copies = to_holders(lambda: planes.at[p], query_send, query_recv, (2, 1))
     fresh_copies = to_holders(lambda: fresh.at[p], fresh_send, fresh_recv)
 
     def plane(ref, k):
@@ -363,7 +363,20 @@
         lax.broadcasted_iota(jnp.int32, (pairs, PLANE), 0) & (KV_HEADS - 1)
     )
     slot_rows = leaving[...].reshape(slots * keep, 2 * PLANE)
-    for copy in query_copies:
+    query_copies[0].wait_recv()
+    beyond = planes.at[partner(p, 2)]
+    query_copies.append(
+        pltpu.make_async_remote_copy(
+            src_ref=beyond,
+            dst_ref=beyond,
+            send_sem=query_send.at[3],
+            recv_sem=query_recv.at[3],
+            device_id=(partner(p, 1), t),
+            device_id_type=MESH,
+        )
+    )
+    query_copies[2].start()
+    for copy in query_copies[1:]:
         copy.wait_recv()
 
     spread = []
@@ -520,7 +533,7 @@
             jax.ShapeDtypeStruct((slots, keep, width), bf16),
         ),
         in_specs=[pinned] * 9,
-        out_specs=(vmem, vmem),
+        out_specs=(vmem, pl.BlockSpec(memory_space=pl.ANY)),
         scratch_shapes=[
             pltpu.VMEM((part, model), bf16),
             pltpu.VMEM((model // 128, 128), f32),

time: 38.5 us -> 38.3 us (level)
  no operation moved by 1% of the time
where the time goes in v7:
time: 38.3 us; the launch traced here: 38.1 us
  Pallas kernels  36.8 us (96%)
  between operations  1.29 us (3%)
    pallas_call x1, Pallas kernels, fused_device(): pl.pallas_call(fused_kernel, out_shape=(jax.ShapeDtypeStruct((requests, H...  34.8 us
    pallas_call x1, Pallas kernels, fused_device(): pl.pallas_call(deliver_kernel, out_shape=(jax.ShapeDtypeStruct(attended.s...  2.06 us

profile of v7, /device:TPU:0, one launch (start us, length us, event | category | flops | bytes accessed | tf_op | source)
XLA Modules:
  0.0 38.1 jit_solution(11376055992328575688)
XLA Ops:
  1.3 34.8 %shard_map.104 = (bf16[64,2560]{1,0:T(8,128)(2,1)}, bf16[8,32,1280]{2,1,0:T(8,128)(2,1)}) custom-call(bf16[4,16,2560]{2,1,0:T(8,128)(2,1)} %bitcast.14, f32[20,128]{1,0:T(8,128)} %bitcast.15, s32[1,1]{1,0:T(1,128)S(6)} %copy.12.count_in, s32[1,8]{1,0:T(1,128)} %bitcast.16, s32[1,8]{1,0:T(1,128)} %bitcast.17, s32[8,1,32]{2,1,0:T(1,128)} %kept_in.1, ...), custom_call_target="tpu_custom_call" | custom-call | flops 1500000000 | bytes 7000000 | tf_op jit(solution)/shard_map/pallas_call | solution.py:529
  36.1 2.1 %shard_map.105 = (bf16[64,2560]{1,0:T(8,128)(2,1)}, bf16[8,32,1280]{2,1,0:T(8,128)(2,1)}) custom-call(bf16[64,2560]{1,0:T(8,128)(2,1)} %get-tuple-element.6.attended, bf16[8,32,1280]{2,1,0:T(8,128)(2,1)} %get-tuple-element.7.compacted), custom_call_target="tpu_custom_call" | custom-call | bytes 1966080 | tf_op jit(solution)/shard_map/pallas_call | solution.py:581
